TPU v7x, 32 devices: a whole 2x2x4 slice. The times are simulated.
32 devices in a mesh: ta: 8 (over y, x, core), xy: 4 (over z).
Axes of the slice: x: 2, y: 2, z: 4, core: 2. Of those that a mesh axis runs over, the one named last changes fastest.
Arguments:
- residual: bfloat16 [8, 32, 2, 2, 12, 128], P('ta', 'xy'), may hold values from -6 to 6
- vectors: bfloat16 [8, 8, 1, 2, 2, 24, 3072], P('ta', 'xy'), may hold values from -0.625 to 0.625
- hopping: bfloat16 [8, 2, 24, 24, 8, 8, 1, 2], P(None, None, None, None, 'ta', 'xy'), may hold values from -0.3125 to 0.3125
- inverse: bfloat16 [2, 24, 24, 8, 8, 1, 2], P(None, None, None, 'ta', 'xy'), may hold values from -0.41 to 1.81
Outputs:
- correction: float32 [8, 32, 2, 2, 12, 128], P('ta', 'xy')
All inputs are finite; a program needn't handle non-finite values.
Results may differ from a plain program's by a relative error of at most 0.0029.
Values may be sent and summed in bfloat16 or wider, within the bound.
A program may use at most 64 MiB of HBM per device.

v0:
```python
import jax
import jax.numpy as jnp
from jax import lax
from jax.sharding import PartitionSpec as P

highest = lax.Precision.HIGHEST


def partner(x, axis, bit):
    return lax.ppermute(x, axis, [(i, i ^ 1 << bit) for i in range(lax.axis_size(axis))])


def shifted(x, axis, by):
    peers = lax.axis_size(axis)
    return lax.ppermute(x, axis, [(i, (i + by) % peers) for i in range(peers)])


def with_halo(cells, sides, width):
    for axis, dim in sides:
        count = lax.axis_size(axis)
        head = lax.slice_in_dim(cells, 0, width, axis=dim)
        tail = lax.slice_in_dim(cells, cells.shape[dim] - width, cells.shape[dim], axis=dim)
        cells = jnp.concatenate(
            [
                lax.ppermute(tail, axis, [(i, (i + 1) % count) for i in range(count)]),
                cells,
                lax.ppermute(head, axis, [((i + 1) % count, i) for i in range(count)]),
            ],
            axis=dim,
        )
    return cells


def complex_apply(matrix, vector_field):
    products = jnp.einsum("pabxzy,xzyrqb->xzyrpqa", matrix, vector_field, precision=highest)
    real_part = products[..., 0, 0, :] - products[..., 1, 1, :]
    imag_part = products[..., 0, 1, :] + products[..., 1, 0, :]
    return jnp.stack((real_part, imag_part), axis=-2)


def regroup(pieces, position, returning):
    stacked = pieces.reshape((2, 2) + pieces.shape[1:])
    for bit_index in (0, 1):
        section_dim = 1 - bit_index
        own_bit = position // (1 << bit_index) % 2
        kept_half = lax.dynamic_index_in_dim(stacked, own_bit, section_dim, keepdims=False)
        sent_half = lax.dynamic_index_in_dim(stacked, 1 - own_bit, section_dim, keepdims=False)
        if returning:
            received = partner(sent_half, "ta", bit_index)
        else:
            received = partner(sent_half, "ta", bit_index)
        lower_half = jnp.where(own_bit == 0, kept_half, received)
        upper_half = jnp.where(own_bit == 0, received, kept_half)
        stacked = jnp.stack((lower_half, upper_half), axis=section_dim)
    return stacked.reshape(pieces.shape)


def hopping_term(link_blocks, vector_field, position):
    z_quarter = position % 4
    outgoing = (
        (-4, vector_field),
        (4, vector_field),
        (-1, vector_field),
        (3, vector_field),
        (1, vector_field),
        (-3, vector_field),
    )
    arrived = []
    for offset, payload in outgoing:
        arrived.append(shifted(payload, "ta", offset))
    next_face = jnp.where(z_quarter == 3, arrived[3], arrived[2])
    prev_face = jnp.where(z_quarter == 0, arrived[5], arrived[4])
    z_next = jnp.concatenate((vector_field[:, 1:], next_face), axis=1)
    z_prev = jnp.concatenate((prev_face, vector_field[:, :-1]), axis=1)
    padded = with_halo(vector_field, (("xy", 0),), 1)
    x_next = padded[2:]
    x_prev = padded[:-2]
    y_next = jnp.roll(vector_field, -1, axis=2)
    y_prev = jnp.roll(vector_field, 1, axis=2)
    neighbours = (arrived[0], arrived[1], z_next, z_prev, x_next, x_prev, y_next, y_prev)
    summed = jnp.zeros_like(vector_field)
    for direction in range(8):
        summed = summed + complex_apply(link_blocks[direction], neighbours[direction])
    return summed


def sweeps(coarse_rhs, link_blocks, blocks, position):
    solution = complex_apply(blocks, coarse_rhs)
    for sweep_index in range(2):
        solution = complex_apply(blocks, coarse_rhs - hopping_term(link_blocks, solution, position))
    return solution


def shards(residual, vectors, hopping, inverse):
    position = lax.axis_index("ta")
    x_blocks = vectors.shape[1]
    z_blocks = vectors.shape[2]
    y_blocks = vectors.shape[3]
    rhs_count = residual.shape[2]
    fine_rows = residual[0].reshape(x_blocks, 4, rhs_count, 2, 12, 4, z_blocks, 4, y_blocks, 4)
    pieces = fine_rows.transpose(5, 0, 6, 8, 2, 3, 4, 7, 1, 9)
    gathered = regroup(pieces, position, False)
    owned_rows = gathered.transpose(1, 2, 3, 4, 5, 6, 0, 7, 8, 9)
    owned_rows = owned_rows.reshape(x_blocks, z_blocks, y_blocks, rhs_count, 2, -1)
    products = jnp.einsum(
        "abcpkf,abcrqf->abcrpqk", vectors[0], owned_rows, preferred_element_type=jnp.float32
    )
    coarse_rhs = jnp.stack(
        (
            products[..., 0, 0, :] + products[..., 1, 1, :],
            products[..., 0, 1, :] - products[..., 1, 0, :],
        ),
        axis=-2,
    )
    hopping_local = hopping[:, :, :, :, 0]
    blocks_local = inverse[:, :, :, 0]
    solution = sweeps(
        coarse_rhs, hopping_local.astype(jnp.float32), blocks_local.astype(jnp.float32), position
    )
    rounded = solution.astype(jnp.bfloat16)
    products = jnp.einsum(
        "abcpkf,abcrqk->abcrpqf", vectors[0], rounded, preferred_element_type=jnp.float32
    )
    real_part = products[:, :, :, :, 0, 0] - products[:, :, :, :, 1, 1]
    imag_part = products[:, :, :, :, 0, 1] + products[:, :, :, :, 1, 0]
    spread_rows = jnp.stack((real_part, imag_part), axis=4)
    spread_rows = spread_rows.reshape(x_blocks, z_blocks, y_blocks, rhs_count, 2, 12, 4, 4, 4, 4)
    outgoing = spread_rows.transpose(6, 0, 1, 2, 3, 4, 5, 7, 8, 9)
    returned = regroup(outgoing, position, True)
    fine_out = returned.transpose(1, 8, 4, 5, 6, 0, 2, 7, 3, 9)
    return fine_out.reshape(1, 4 * x_blocks, rhs_count, 2, 12, -1)


def solution(mesh):
    placed = (
        P("ta", "xy", None, None, None, None),
        P("ta", "xy", None, None, None, None, None),
        P(None, None, None, None, "ta", "xy", None, None),
        P(None, None, None, "ta", "xy", None, None),
    )
    return jax.shard_map(
        shards,
        mesh=mesh,
        in_specs=placed,
        out_specs=P("ta", "xy", None, None, None, None),
        check_vma=False,
    )
```

profile of v0, /device:TPU:0, one launch (start us, length us, event | category | flops | bytes accessed | tf_op | source)
XLA Modules:
  0.0 133.5 jit_solution(9963374838009031020)
XLA Ops:
  0.0 1.5 %copy.199 = bf16[1,8,2,2,12,128]{4,5,3,2,1,0:T(8,128)(2,1)S(1)} copy(bf16[1,8,2,2,12,128]{5,3,4,2,1,0:T(2,128)(2,1)} %param.4) | data formatting | bytes 196608 | tf_op args[0]
  2.9 1.5 %collective-permute-done = bf16[2,2,1,2,2,2,12,4,4,4]{6,9,8,7,5,4,3,1,0,2:T(4,128)(2,1)S(1)} collective-permute-done((bf16[2,2,1,2,2,2,12,4,4,4]{6,9,8,7,5,4,3,1,0,2:T(4,128)(2,1)S(1)}, bf16[2,2,1,2,2,2,12,4,4,4]{6,9,8,7,5,4,3,1,0,2:T(4,128)(2,1)S(1)}, u32[]{:S(2)}, u32[]{:S(2)}) %collective-permute-start) | collective-permute-done | bytes 49184 | tf_op jit(solution)/shard_map/ppermute | solution.py:10
  5.4 2.9 %collective-permute-start.1 = (bf16[2,2,1,2,2,2,12,4,4,4]{6,9,8,7,5,4,3,1,0,2:T(4,128)(2,1)S(1)}, bf16[2,2,1,2,2,2,12,4,4,4]{6,9,8,7,5,4,3,1,0,2:T(4,128)(2,1)S(1)}, u32[]{:S(2)}, u32[]{:S(2)}) collective-permute-start(bf16[2,2,1,2,2,2,12,4,4,4]{6,9,8,7,5,4,3,1,0,2:T(4,128)(2,1)S(1)} %fusion.12), channel_id=1, source_target_pairs={{0,8},{4,12},{8,0},{12,4},{16,24},{20,28},{24,16},{28,20},{1,9},{5... | collective-permute-start | bytes 147464 | tf_op jit(solution)/shard_map/ppermute | solution.py:10
  9.3 11.3 %collective-permute-done.1 = bf16[2,2,1,2,2,2,12,4,4,4]{6,9,8,7,5,4,3,1,0,2:T(4,128)(2,1)S(1)} collective-permute-done((bf16[2,2,1,2,2,2,12,4,4,4]{6,9,8,7,5,4,3,1,0,2:T(4,128)(2,1)S(1)}, bf16[2,2,1,2,2,2,12,4,4,4]{6,9,8,7,5,4,3,1,0,2:T(4,128)(2,1)S(1)}, u32[]{:S(2)}, u32[]{:S(2)}) %collective-permute-start.1) | collective-permute-done | bytes 49184 | tf_op jit(solution)/shard_map/ppermute | solution.py:10
  22.2 9.4 %copy.206 = bf16[4,2,1,2,2,2,12,4,4,4]{9,8,7,0,6,5,4,3,1,2:T(4,128)(2,1)} copy(bf16[4,2,1,2,2,2,12,4,4,4]{6,9,8,7,5,4,3,1,0,2:T(4,128)(2,1)S(1)} %bitcast.421) | data formatting | bytes 196608 | tf_op jit(solution)/shard_map/reshape | solution.py:55
  31.6 6.9 %reshape.1446 = bf16[2,2,2,2,3072,1]{4,3,2,1,0,5:T(2,128)(2,1)S(1)} reshape(bf16[2,1,2,2,2,12,4,4,4,4]{9,8,7,6,5,4,3,2,0,1:T(4,128)(2,1)} %bitcast.416) | data formatting | bytes 196608 | tf_op jit(solution)/shard_map/reshape
  40.1 3.0 %collective-permute-start.5 = (f32[2,1,2,2,2,24]{5,3,2,0,4,1:T(2,128)S(1)}, f32[2,1,2,2,2,24]{5,3,2,0,4,1:T(2,128)S(1)}, u32[]{:S(2)}, u32[]{:S(2)}) collective-permute-start(f32[2,1,2,2,2,24]{5,3,2,0,4,1:T(2,128)S(1)} %pad_maximum_fusion.3), channel_id=1, source_target_pairs={{0,20},{4,24},{8,28},{12,0},{16,4},{20,8},{24,12},{28,16},{1,21},{... | collective-permute-start | bytes 4616 | tf_op jit(solution)/shard_map/ppermute | solution.py:15
  43.5 1.8 %collective-permute-start.8 = (f32[1,1,2,2,2,24]{5,3,2,0,4,1:T(2,128)S(1)}, f32[1,1,2,2,2,24]{5,3,2,0,4,1:T(2,128)S(1)}, u32[]{:S(2)}, u32[]{:S(2)}) collective-permute-start(f32[1,1,2,2,2,24]{5,3,2,0,4,1:T(2,128)S(1)} %get-tuple-element.73), channel_id=1, source_target_pairs={{0,1},{1,2},{2,3},{3,0},{4,5},{5,6},{6,7},{7,4},{8,9},{9,10},{10,1... | collective-permute-start | bytes 2312 | tf_op jit(solution)/shard_map/ppermute | solution.py:25
  46.0 2.9 %collective-permute-done.8 = f32[1,1,2,2,2,24]{5,3,2,0,4,1:T(2,128)S(1)} collective-permute-done((f32[1,1,2,2,2,24]{5,3,2,0,4,1:T(2,128)S(1)}, f32[1,1,2,2,2,24]{5,3,2,0,4,1:T(2,128)S(1)}, u32[]{:S(2)}, u32[]{:S(2)}) %collective-permute-start.8) | collective-permute-done | bytes 800 | tf_op jit(solution)/shard_map/ppermute | solution.py:25
  48.9 2.1 %collective-permute-start.7 = (f32[1,1,2,2,2,24]{5,3,2,0,4,1:T(2,128)S(1)}, f32[1,1,2,2,2,24]{5,3,2,0,4,1:T(2,128)S(1)}, u32[]{:S(2)}, u32[]{:S(2)}) collective-permute-start(f32[1,1,2,2,2,24]{5,3,2,0,4,1:T(2,128)S(1)} %get-tuple-element.74), channel_id=1, source_target_pairs={{1,0},{2,1},{3,2},{0,3},{5,4},{6,5},{7,6},{4,7},{9,8},{10,9},{11,1... | collective-permute-start | bytes 2312 | tf_op jit(solution)/shard_map/ppermute | solution.py:27
  52.5 1.7 %collective-permute-start.2 = (f32[2,1,2,2,2,24]{5,3,2,0,4,1:T(2,128)S(1)}, f32[2,1,2,2,2,24]{5,3,2,0,4,1:T(2,128)S(1)}, u32[]{:S(2)}, u32[]{:S(2)}) collective-permute-start(f32[2,1,2,2,2,24]{5,3,2,0,4,1:T(2,128)S(1)} %pad_maximum_fusion.3), channel_id=1, source_target_pairs={{0,16},{4,20},{8,24},{12,28},{16,0},{20,4},{24,8},{28,12},{1,17},{... | collective-permute-start | bytes 4616 | tf_op jit(solution)/shard_map/ppermute | solution.py:15
  58.1 2.9 %collective-permute-start.12 = (f32[2,1,2,2,2,24]{5,3,2,0,4,1:T(2,128)S(1)}, f32[2,1,2,2,2,24]{5,3,2,0,4,1:T(2,128)S(1)}, u32[]{:S(2)}, u32[]{:S(2)}) collective-permute-start(f32[2,1,2,2,2,24]{5,3,2,0,4,1:T(2,128)S(1)} %pad_maximum_fusion.4), channel_id=1, source_target_pairs={{0,20},{4,24},{8,28},{12,0},{16,4},{20,8},{24,12},{28,16},{1,21},{... | collective-permute-start | bytes 4616 | tf_op jit(solution)/shard_map/ppermute | solution.py:15
  61.4 3.9 %collective-permute-start.14 = (f32[1,1,2,2,2,24]{5,3,2,0,4,1:T(2,128)S(1)}, f32[1,1,2,2,2,24]{5,3,2,0,4,1:T(2,128)S(1)}, u32[]{:S(2)}, u32[]{:S(2)}) collective-permute-start(f32[1,1,2,2,2,24]{5,3,2,0,4,1:T(2,128)S(1)} %get-tuple-element.67), channel_id=1, source_target_pairs={{1,0},{2,1},{3,2},{0,3},{5,4},{6,5},{7,6},{4,7},{9,8},{10,9},{11,1... | collective-permute-start | bytes 2312 | tf_op jit(solution)/shard_map/ppermute | solution.py:27
  65.3 1.3 collective-permute-done.14
  67.0 5.3 %collective-permute-done.15 = f32[1,1,2,2,2,24]{5,3,2,0,4,1:T(2,128)S(1)} collective-permute-done((f32[1,1,2,2,2,24]{5,3,2,0,4,1:T(2,128)S(1)}, f32[1,1,2,2,2,24]{5,3,2,0,4,1:T(2,128)S(1)}, u32[]{:S(2)}, u32[]{:S(2)}) %collective-permute-start.15) | collective-permute-done | bytes 800 | tf_op jit(solution)/shard_map/ppermute | solution.py:25
  72.3 1.5 %collective-permute-start.9 = (f32[2,1,2,2,2,24]{5,3,2,0,4,1:T(2,128)S(1)}, f32[2,1,2,2,2,24]{5,3,2,0,4,1:T(2,128)S(1)}, u32[]{:S(2)}, u32[]{:S(2)}) collective-permute-start(f32[2,1,2,2,2,24]{5,3,2,0,4,1:T(2,128)S(1)} %pad_maximum_fusion.4), channel_id=1, source_target_pairs={{0,16},{4,20},{8,24},{12,28},{16,0},{20,4},{24,8},{28,12},{1,17},{... | collective-permute-start | bytes 4616 | tf_op jit(solution)/shard_map/ppermute | solution.py:15
  78.2 5.8 %sub.418 = f32[2,1,2,2,1,12,4,4,4,4]{9,8,7,6,5,3,2,0,4,1:T(4,128)} reshape(f32[2,2,2,3072]{3,2,1,0:T(2,128)S(1)} %get-tuple-element.5) | data formatting | bytes 196608 | tf_op jit(solution)/shard_map/sub | solution.py:124
  83.9 5.0 %copy.260 = f32[2,1,2,2,1,12,4,4,4,4]{5,9,8,7,6,4,3,2,1,0:T(4,128)S(1)} copy(f32[2,1,2,2,1,12,4,4,4,4]{9,8,7,6,5,3,2,0,4,1:T(4,128)} %sub.418) | data formatting | bytes 196608 | tf_op jit(solution)/shard_map/sub | solution.py:124
  88.9 5.8 %add.528 = f32[2,1,2,2,1,12,4,4,4,4]{9,8,7,6,5,3,2,0,4,1:T(4,128)} reshape(f32[2,2,2,3072]{3,2,1,0:T(2,128)S(1)} %get-tuple-element.6) | data formatting | bytes 196608 | tf_op jit(solution)/shard_map/add | solution.py:125
  94.7 5.0 %copy.261 = f32[2,1,2,2,1,12,4,4,4,4]{5,9,8,7,6,4,3,2,1,0:T(4,128)S(1)} copy(f32[2,1,2,2,1,12,4,4,4,4]{9,8,7,6,5,3,2,0,4,1:T(4,128)} %add.528) | data formatting | bytes 196608 | tf_op jit(solution)/shard_map/add | solution.py:125
  101.0 2.6 %collective-permute-done.16 = f32[2,2,1,2,2,2,12,4,4,4]{6,9,8,7,5,4,3,1,0,2:T(4,128)S(1)} collective-permute-done((f32[2,2,1,2,2,2,12,4,4,4]{6,9,8,7,5,4,3,1,0,2:T(4,128)S(1)}, f32[2,2,1,2,2,2,12,4,4,4]{6,9,8,7,5,4,3,1,0,2:T(4,128)S(1)}, u32[]{:S(2)}, u32[]{:S(2)}) %collective-permute-start.16) | collective-permute-done | bytes 98336 | tf_op jit(solution)/shard_map/ppermute | solution.py:10
  104.5 1.5 %collective-permute-start.17 = (f32[2,2,1,2,2,2,12,4,4,4]{6,9,8,7,5,4,3,1,0,2:T(4,128)S(1)}, f32[2,2,1,2,2,2,12,4,4,4]{6,9,8,7,5,4,3,1,0,2:T(4,128)S(1)}, u32[]{:S(2)}, u32[]{:S(2)}) collective-permute-start(f32[2,2,1,2,2,2,12,4,4,4]{6,9,8,7,5,4,3,1,0,2:T(4,128)S(1)} %fusion.7), channel_id=1, source_target_pairs={{0,8},{4,12},{8,0},{12,4},{16,24},{20,28},{24,16},{28,20},{1,9},{5... | collective-permute-start | bytes 294920 | tf_op jit(solution)/shard_map/ppermute | solution.py:10
  106.0 23.7 %collective-permute-done.17 = f32[2,2,1,2,2,2,12,4,4,4]{6,9,8,7,5,4,3,1,0,2:T(4,128)S(1)} collective-permute-done((f32[2,2,1,2,2,2,12,4,4,4]{6,9,8,7,5,4,3,1,0,2:T(4,128)S(1)}, f32[2,2,1,2,2,2,12,4,4,4]{6,9,8,7,5,4,3,1,0,2:T(4,128)S(1)}, u32[]{:S(2)}, u32[]{:S(2)}) %collective-permute-start.17) | collective-permute-done | bytes 98336 | tf_op jit(solution)/shard_map/ppermute | solution.py:10
  132.2 1.3 copy.268
  (98 shorter events, 22.5 us)
Async XLA Ops:
  0.0 38.4 %copy-start = (bf16[1,2,1,2,2,24,3072]{6,5,4,3,2,1,0:T(8,128)(2,1)S(1)}, bf16[1,2,1,2,2,24,3072]{6,5,4,3,2,1,0:T(8,128)(2,1)}, u32[]{:S(2)}) copy-start(bf16[1,2,1,2,2,24,3072]{6,5,4,3,2,1,0:T(8,128)(2,1)} %param.5) | copy-start | bytes 3538948
  2.4 2.1 %collective-permute-start = (bf16[2,2,1,2,2,2,12,4,4,4]{6,9,8,7,5,4,3,1,0,2:T(4,128)(2,1)S(1)}, bf16[2,2,1,2,2,2,12,4,4,4]{6,9,8,7,5,4,3,1,0,2:T(4,128)(2,1)S(1)}, u32[]{:S(2)}, u32[]{:S(2)}) collective-permute-start(bf16[2,2,1,2,2,2,12,4,4,4]{6,9,8,7,5,4,3,1,0,2:T(4,128)(2,1)S(1)} %bitcast.423), channel_id=1, source_target_pairs={{0,4},{4,0},{8,12},{12,8},{16,20},{20,16},{24,28},{28,24},{1,5},{5... | collective-permute-start | bytes 147464 | tf_op jit(solution)/shard_map/ppermute | solution.py:10
  4.4 3.9 %copy-start.1 = (bf16[8,2,24,24,1,2,1,2]{3,7,6,5,4,2,1,0:T(2,128)(2,1)S(1)}, bf16[8,2,24,24,1,2,1,2]{3,7,6,5,4,2,1,0:T(2,128)(2,1)}, u32[]{:S(2)}) copy-start(bf16[8,2,24,24,1,2,1,2]{3,7,6,5,4,2,1,0:T(2,128)(2,1)} %param.6) | copy-start | bytes 221188
  5.4 15.1 %collective-permute-start.1 = (bf16[2,2,1,2,2,2,12,4,4,4]{6,9,8,7,5,4,3,1,0,2:T(4,128)(2,1)S(1)}, bf16[2,2,1,2,2,2,12,4,4,4]{6,9,8,7,5,4,3,1,0,2:T(4,128)(2,1)S(1)}, u32[]{:S(2)}, u32[]{:S(2)}) collective-permute-start(bf16[2,2,1,2,2,2,12,4,4,4]{6,9,8,7,5,4,3,1,0,2:T(4,128)(2,1)S(1)} %fusion.12), channel_id=1, source_target_pairs={{0,8},{4,12},{8,0},{12,4},{16,24},{20,28},{24,16},{28,20},{1,9},{5... | collective-permute-start | bytes 147464 | tf_op jit(solution)/shard_map/ppermute | solution.py:10
  31.6 8.1 %copy-start.2 = (bf16[2,24,24,1,2,1,2]{2,6,5,4,3,1,0:T(2,128)(2,1)S(1)}, bf16[2,24,24,1,2,1,2]{2,6,5,4,3,1,0:T(2,128)(2,1)}, u32[]{:S(2)}) copy-start(bf16[2,24,24,1,2,1,2]{2,6,5,4,3,1,0:T(2,128)(2,1)} %param.7) | copy-start | bytes 27652
  31.6 13.7 %copy-start.5 = (bf16[1,2,24,24,1,2,1,2]{3,7,6,5,4,2,1,0:T(2,128)(2,1)S(1)}, bf16[1,2,24,24,1,2,1,2]{3,7,6,5,4,2,1,0:T(2,128)(2,1)}, u32[]{:S(2)}) copy-start(bf16[1,2,24,24,1,2,1,2]{3,7,6,5,4,2,1,0:T(2,128)(2,1)} %get-tuple-element.24) | copy-start | bytes 27652
  31.6 14.1 %copy-start.4 = (bf16[1,2,24,24,1,2,1,2]{3,7,6,5,4,2,1,0:T(2,128)(2,1)S(1)}, bf16[1,2,24,24,1,2,1,2]{3,7,6,5,4,2,1,0:T(2,128)(2,1)}, u32[]{:S(2)}) copy-start(bf16[1,2,24,24,1,2,1,2]{3,7,6,5,4,2,1,0:T(2,128)(2,1)} %get-tuple-element.17) | copy-start | bytes 27652
  31.6 22.7 %copy-start.3 = (bf16[1,2,24,24,1,2,1,2]{3,7,6,5,4,2,1,0:T(2,128)(2,1)S(1)}, bf16[1,2,24,24,1,2,1,2]{3,7,6,5,4,2,1,0:T(2,128)(2,1)}, u32[]{:S(2)}) copy-start(bf16[1,2,24,24,1,2,1,2]{3,7,6,5,4,2,1,0:T(2,128)(2,1)} %get-tuple-element.19) | copy-start | bytes 27652
  40.1 14.5 %collective-permute-start.6 = (f32[2,1,2,2,2,24]{5,3,2,0,4,1:T(2,128)S(1)}, f32[2,1,2,2,2,24]{5,3,2,0,4,1:T(2,128)S(1)}, u32[]{:S(2)}, u32[]{:S(2)}) collective-permute-start(f32[2,1,2,2,2,24]{5,3,2,0,4,1:T(2,128)S(1)} %pad_maximum_fusion.3), channel_id=1, source_target_pairs={{0,4},{4,8},{8,12},{12,16},{16,20},{20,24},{24,28},{28,0},{1,5},{5... | collective-permute-start | bytes 4616 | tf_op jit(solution)/shard_map/ppermute | solution.py:15
  40.1 14.5 %collective-permute-start.5 = (f32[2,1,2,2,2,24]{5,3,2,0,4,1:T(2,128)S(1)}, f32[2,1,2,2,2,24]{5,3,2,0,4,1:T(2,128)S(1)}, u32[]{:S(2)}, u32[]{:S(2)}) collective-permute-start(f32[2,1,2,2,2,24]{5,3,2,0,4,1:T(2,128)S(1)} %pad_maximum_fusion.3), channel_id=1, source_target_pairs={{0,20},{4,24},{8,28},{12,0},{16,4},{20,8},{24,12},{28,16},{1,21},{... | collective-permute-start | bytes 4616 | tf_op jit(solution)/shard_map/ppermute | solution.py:15
  43.1 11.9 %collective-permute-start.4 = (f32[2,1,2,2,2,24]{5,3,2,0,4,1:T(2,128)S(1)}, f32[2,1,2,2,2,24]{5,3,2,0,4,1:T(2,128)S(1)}, u32[]{:S(2)}, u32[]{:S(2)}) collective-permute-start(f32[2,1,2,2,2,24]{5,3,2,0,4,1:T(2,128)S(1)} %pad_maximum_fusion.3), channel_id=1, source_target_pairs={{0,28},{4,0},{8,4},{12,8},{16,12},{20,16},{24,20},{28,24},{1,29},{... | collective-permute-start | bytes 4616 | tf_op jit(solution)/shard_map/ppermute | solution.py:15
  43.2 11.9 %collective-permute-start.3 = (f32[2,1,2,2,2,24]{5,3,2,0,4,1:T(2,128)S(1)}, f32[2,1,2,2,2,24]{5,3,2,0,4,1:T(2,128)S(1)}, u32[]{:S(2)}, u32[]{:S(2)}) collective-permute-start(f32[2,1,2,2,2,24]{5,3,2,0,4,1:T(2,128)S(1)} %pad_maximum_fusion.3), channel_id=1, source_target_pairs={{0,12},{4,16},{8,20},{12,24},{16,28},{20,0},{24,4},{28,8},{1,13},{... | collective-permute-start | bytes 4616 | tf_op jit(solution)/shard_map/ppermute | solution.py:15
  43.5 5.4 %collective-permute-start.8 = (f32[1,1,2,2,2,24]{5,3,2,0,4,1:T(2,128)S(1)}, f32[1,1,2,2,2,24]{5,3,2,0,4,1:T(2,128)S(1)}, u32[]{:S(2)}, u32[]{:S(2)}) collective-permute-start(f32[1,1,2,2,2,24]{5,3,2,0,4,1:T(2,128)S(1)} %get-tuple-element.73), channel_id=1, source_target_pairs={{0,1},{1,2},{2,3},{3,0},{4,5},{5,6},{6,7},{7,4},{8,9},{9,10},{10,1... | collective-permute-start | bytes 2312 | tf_op jit(solution)/shard_map/ppermute | solution.py:25
  48.9 3.6 %collective-permute-start.7 = (f32[1,1,2,2,2,24]{5,3,2,0,4,1:T(2,128)S(1)}, f32[1,1,2,2,2,24]{5,3,2,0,4,1:T(2,128)S(1)}, u32[]{:S(2)}, u32[]{:S(2)}) collective-permute-start(f32[1,1,2,2,2,24]{5,3,2,0,4,1:T(2,128)S(1)} %get-tuple-element.74), channel_id=1, source_target_pairs={{1,0},{2,1},{3,2},{0,3},{5,4},{6,5},{7,6},{4,7},{9,8},{10,9},{11,1... | collective-permute-start | bytes 2312 | tf_op jit(solution)/shard_map/ppermute | solution.py:27
  52.5 3.7 %collective-permute-start.2 = (f32[2,1,2,2,2,24]{5,3,2,0,4,1:T(2,128)S(1)}, f32[2,1,2,2,2,24]{5,3,2,0,4,1:T(2,128)S(1)}, u32[]{:S(2)}, u32[]{:S(2)}) collective-permute-start(f32[2,1,2,2,2,24]{5,3,2,0,4,1:T(2,128)S(1)} %pad_maximum_fusion.3), channel_id=1, source_target_pairs={{0,16},{4,20},{8,24},{12,28},{16,0},{20,4},{24,8},{28,12},{1,17},{... | collective-permute-start | bytes 4616 | tf_op jit(solution)/shard_map/ppermute | solution.py:15
  58.1 16.1 %collective-permute-start.13 = (f32[2,1,2,2,2,24]{5,3,2,0,4,1:T(2,128)S(1)}, f32[2,1,2,2,2,24]{5,3,2,0,4,1:T(2,128)S(1)}, u32[]{:S(2)}, u32[]{:S(2)}) collective-permute-start(f32[2,1,2,2,2,24]{5,3,2,0,4,1:T(2,128)S(1)} %pad_maximum_fusion.4), channel_id=1, source_target_pairs={{0,4},{4,8},{8,12},{12,16},{16,20},{20,24},{24,28},{28,0},{1,5},{5... | collective-permute-start | bytes 4616 | tf_op jit(solution)/shard_map/ppermute | solution.py:15
  58.1 16.0 %collective-permute-start.12 = (f32[2,1,2,2,2,24]{5,3,2,0,4,1:T(2,128)S(1)}, f32[2,1,2,2,2,24]{5,3,2,0,4,1:T(2,128)S(1)}, u32[]{:S(2)}, u32[]{:S(2)}) collective-permute-start(f32[2,1,2,2,2,24]{5,3,2,0,4,1:T(2,128)S(1)} %pad_maximum_fusion.4), channel_id=1, source_target_pairs={{0,20},{4,24},{8,28},{12,0},{16,4},{20,8},{24,12},{28,16},{1,21},{... | collective-permute-start | bytes 4616 | tf_op jit(solution)/shard_map/ppermute | solution.py:15
  61.1 13.5 %collective-permute-start.11 = (f32[2,1,2,2,2,24]{5,3,2,0,4,1:T(2,128)S(1)}, f32[2,1,2,2,2,24]{5,3,2,0,4,1:T(2,128)S(1)}, u32[]{:S(2)}, u32[]{:S(2)}) collective-permute-start(f32[2,1,2,2,2,24]{5,3,2,0,4,1:T(2,128)S(1)} %pad_maximum_fusion.4), channel_id=1, source_target_pairs={{0,28},{4,0},{8,4},{12,8},{16,12},{20,16},{24,20},{28,24},{1,29},{... | collective-permute-start | bytes 4616 | tf_op jit(solution)/shard_map/ppermute | solution.py:15
  61.1 13.5 %collective-permute-start.10 = (f32[2,1,2,2,2,24]{5,3,2,0,4,1:T(2,128)S(1)}, f32[2,1,2,2,2,24]{5,3,2,0,4,1:T(2,128)S(1)}, u32[]{:S(2)}, u32[]{:S(2)}) collective-permute-start(f32[2,1,2,2,2,24]{5,3,2,0,4,1:T(2,128)S(1)} %pad_maximum_fusion.4), channel_id=1, source_target_pairs={{0,12},{4,16},{8,20},{12,24},{16,28},{20,0},{24,4},{28,8},{1,13},{... | collective-permute-start | bytes 4616 | tf_op jit(solution)/shard_map/ppermute | solution.py:15
  61.4 5.2 %collective-permute-start.14 = (f32[1,1,2,2,2,24]{5,3,2,0,4,1:T(2,128)S(1)}, f32[1,1,2,2,2,24]{5,3,2,0,4,1:T(2,128)S(1)}, u32[]{:S(2)}, u32[]{:S(2)}) collective-permute-start(f32[1,1,2,2,2,24]{5,3,2,0,4,1:T(2,128)S(1)} %get-tuple-element.67), channel_id=1, source_target_pairs={{1,0},{2,1},{3,2},{0,3},{5,4},{6,5},{7,6},{4,7},{9,8},{10,9},{11,1... | collective-permute-start | bytes 2312 | tf_op jit(solution)/shard_map/ppermute | solution.py:27
  66.6 5.7 %collective-permute-start.15 = (f32[1,1,2,2,2,24]{5,3,2,0,4,1:T(2,128)S(1)}, f32[1,1,2,2,2,24]{5,3,2,0,4,1:T(2,128)S(1)}, u32[]{:S(2)}, u32[]{:S(2)}) collective-permute-start(f32[1,1,2,2,2,24]{5,3,2,0,4,1:T(2,128)S(1)} %get-tuple-element.68), channel_id=1, source_target_pairs={{0,1},{1,2},{2,3},{3,0},{4,5},{5,6},{6,7},{7,4},{8,9},{9,10},{10,1... | collective-permute-start | bytes 2312 | tf_op jit(solution)/shard_map/ppermute | solution.py:25
  72.3 3.7 %collective-permute-start.9 = (f32[2,1,2,2,2,24]{5,3,2,0,4,1:T(2,128)S(1)}, f32[2,1,2,2,2,24]{5,3,2,0,4,1:T(2,128)S(1)}, u32[]{:S(2)}, u32[]{:S(2)}) collective-permute-start(f32[2,1,2,2,2,24]{5,3,2,0,4,1:T(2,128)S(1)} %pad_maximum_fusion.4), channel_id=1, source_target_pairs={{0,16},{4,20},{8,24},{12,28},{16,0},{20,4},{24,8},{28,12},{1,17},{... | collective-permute-start | bytes 4616 | tf_op jit(solution)/shard_map/ppermute | solution.py:15
  100.9 2.7 %collective-permute-start.16 = (f32[2,2,1,2,2,2,12,4,4,4]{6,9,8,7,5,4,3,1,0,2:T(4,128)S(1)}, f32[2,2,1,2,2,2,12,4,4,4]{6,9,8,7,5,4,3,1,0,2:T(4,128)S(1)}, u32[]{:S(2)}, u32[]{:S(2)}) collective-permute-start(f32[2,2,1,2,2,2,12,4,4,4]{6,9,8,7,5,4,3,1,0,2:T(4,128)S(1)} %bitcast.422), channel_id=1, source_target_pairs={{0,4},{4,0},{8,12},{12,8},{16,20},{20,16},{24,28},{28,24},{1,5},{5... | collective-permute-start | bytes 294920 | tf_op jit(solution)/shard_map/ppermute | solution.py:10
  104.5 25.3 %collective-permute-start.17 = (f32[2,2,1,2,2,2,12,4,4,4]{6,9,8,7,5,4,3,1,0,2:T(4,128)S(1)}, f32[2,2,1,2,2,2,12,4,4,4]{6,9,8,7,5,4,3,1,0,2:T(4,128)S(1)}, u32[]{:S(2)}, u32[]{:S(2)}) collective-permute-start(f32[2,2,1,2,2,2,12,4,4,4]{6,9,8,7,5,4,3,1,0,2:T(4,128)S(1)} %fusion.7), channel_id=1, source_target_pairs={{0,8},{4,12},{8,0},{12,4},{16,24},{20,28},{24,16},{28,20},{1,9},{5... | collective-permute-start | bytes 294920 | tf_op jit(solution)/shard_map/ppermute | solution.py:10
where the time goes:
time: 134 us
  waiting for transfers between devices  51.6 us (39%)
  local copies, waits for them, and re-layouts  43.5 us (32%)
  starting transfers between devices  22.7 us (17%)
  matrix products  8.23 us (6%)
  other arithmetic  6.9 us (5%)
    ppermute x4, waiting for transfers between devices, partner(): lax.ppermute(x, axis, [(i, i ^ 1 << bit) for i in range(lax.axis_size(axi...  39.2 us
    sub x2, local copies, waits for them, and re-layouts, shards(): real_part = products[:, :, :, :, 0, 0] - products[:, :, :, :, 1, 1]  10.8 us
    add x2, local copies, waits for them, and re-layouts, shards(): imag_part = products[:, :, :, :, 0, 1] + products[:, :, :, :, 1, 0]  10.8 us
    reshape x2, local copies, waits for them, and re-layouts, regroup(): return stacked.reshape(pieces.shape)  9.99 us
    ppermute x10, starting transfers between devices, shifted(): return lax.ppermute(x, axis, [(i, (i + by) % peers) for i in range(peers)])  9.96 us
    ppermute x2, waiting for transfers between devices, with_halo(): lax.ppermute(tail, axis, [(i, (i + 1) % count) for i in range(count)])  8.14 us
    reshape x1, local copies, waits for them, and re-layouts  6.86 us
    dot_general x19, matrix products, complex_apply(): jnp.einsum('pabxzy,xzyrqb->xzyrpqa', matrix, vector_field, precision=high...  6.74 us
  transfers between devices with their start and end apart: 18, of which 10 were waited for; matrix products, arithmetic and copies ran while one was open for 3% of the time, Pallas kernels for 0%

commit v1 on v0

v1 whole, which is shorter than its diff:
```python
import functools

import jax
import jax.numpy as jnp
from jax import lax
from jax.experimental import pallas as pl
from jax.experimental.pallas import tpu as pltpu
from jax.sharding import PartitionSpec as P

F32 = jnp.float32
BF16 = jnp.bfloat16
NT = (((1,), (1,)), ((), ()))
MESH = pl.DeviceIdType.MESH


def dot(a, b):
    return jnp.dot(a, b, preferred_element_type=F32)


def dot_nt(a, b):
    return lax.dot_general(a, b, NT, preferred_element_type=F32)


def lanes(rows):
    return lax.broadcasted_iota(jnp.int32, (rows, 128), 1)


def ahead(x, by):
    return pltpu.roll(x, 128 - by, 1)


def behind(x, by):
    return pltpu.roll(x, by, 1)


def swap(x, lane, bit):
    return jnp.where((lane & bit) == 0, ahead(x, bit), behind(x, bit))


def times_i(x, lane):
    return jnp.where((lane & 4) == 0, -ahead(x, 4), behind(x, 4))


def own_site(x_of_site, lane):
    site = (lane & 2) + ((lane >> 3) & 1)
    total = jnp.where(site == 0, x_of_site(0), 0.0)
    for s in range(1, 4):
        total = total + jnp.where(site == s, x_of_site(s), 0.0)
    return total


def spread_groups(x):
    for by in (64, 32, 16):
        x = x + pltpu.roll(x, by, 1)
    return x


def split_field(v, lane):
    high = v.astype(BF16).astype(F32)
    base = jnp.where((lane & 16) == 0, high, v - high)
    return jnp.where((lane & 32) == 0, base, times_i(base, lane))


def pad_rows(w):
    return jnp.concatenate([w, jnp.zeros((8, 128), F32)], axis=0).astype(BF16)


def kernel(
    n_ta,
    n_xy,
    res_hbm,
    vec_hbm,
    hop_hbm,
    inv_hbm,
    out_ref,
    res,
    vec,
    hop,
    inv,
    perm,
    send_in,
    recv_in,
    halo_out,
    halo_in,
    send_back,
    recv_back,
    rows_ref,
    load_sem,
    in_send,
    in_recv,
    halo_send,
    halo_recv,
    back_send,
    back_recv,
):
    ta = lax.axis_index("ta")
    xy = lax.axis_index("xy")
    q = ta % 4
    base = ta - q
    n_t = n_ta // 4

    loads = []
    for i, (src, dst) in enumerate(((res_hbm, res), (vec_hbm, vec), (hop_hbm, hop), (inv_hbm, inv))):
        copy = pltpu.make_async_copy(src, dst, load_sem.at[i])
        copy.start()
        loads.append(copy)

    t_up = (ta + 4) % n_ta
    t_down = (ta + n_ta - 4) % n_ta
    x_up = (xy + 1) % n_xy
    x_down = (xy + n_xy - 1) % n_xy
    mates = [base + (q + j) % 4 for j in (1, 2, 3)]
    greeted = [(mate, xy) for mate in mates] + [(ta, x_up), (ta, x_down), (t_up, xy)]
    if n_t > 2:
        greeted.append((t_down, xy))
    barrier = pltpu.get_barrier_semaphore()
    for device in greeted:
        pl.semaphore_signal(barrier, inc=1, device_id=device, device_id_type=MESH)

    row128 = lax.broadcasted_iota(jnp.int32, (128, 128), 0)
    col128 = lanes(128)
    target = (row128 >> 5) * 128 + ((row128 >> 2) & 1) * 64 + ((row128 >> 3) & 3) * 16 + (row128 & 3)
    offset = target - col128
    for xi in range(4):
        for zq in range(4):
            perm[128 * xi : 128 * xi + 128, 128 * zq : 128 * zq + 128] = jnp.where(
                offset == 128 * zq - 4 * xi, 1.0, 0.0
            ).astype(BF16)
    r96 = lax.broadcasted_iota(jnp.int32, (96, 96), 0)
    c96 = lax.broadcasted_iota(jnp.int32, (96, 96), 1)

    def fine_row(i):
        return ((i >> 1) & 1) * 48 + (i & 1) * 24 + (i >> 3) * 2 + ((i >> 2) & 1)

    gather = jnp.where(c96 == fine_row(r96), 1.0, 0.0).astype(BF16)
    scatter = jnp.where(r96 == fine_row(c96), 1.0, 0.0).astype(BF16)

    loads[0].wait()
    wide = jnp.concatenate(
        [
            jnp.concatenate([res[4 * xc + xi] for xi in range(4)], axis=1)
            for xc in range(2)
        ],
        axis=0,
    )
    sorted_rows = dot(wide, perm[...]).astype(BF16)
    for zq in range(4):
        send_in[zq] = sorted_rows[:, 128 * zq : 128 * zq + 128]

    pl.semaphore_wait(barrier, len(greeted))

    def exchange(src, dst, send_sem, recv_sem):
        copies = []
        for j in (2, 3, 1):
            slot = (q + j) % 4
            copy = pltpu.make_async_remote_copy(
                src_ref=src.at[slot],
                dst_ref=dst.at[q],
                send_sem=send_sem.at[j - 1],
                recv_sem=recv_sem.at[j - 1],
                device_id=(base + slot, xy),
                device_id_type=MESH,
            )
            copy.start()
            copies.append(copy)
        dst[pl.ds(q, 1)] = src[pl.ds(q, 1)]
        return copies

    copies_in = exchange(send_in, recv_in, in_send, in_recv)
    loads[1].wait()
    loads[2].wait()
    loads[3].wait()
    for copy in copies_in:
        copy.wait()

    lane96 = lanes(96)
    lane24 = lanes(24)
    low96 = lane96 < 64
    gathered = [dot(gather, recv_in[ti]) for ti in range(4)]
    turned = [pltpu.roll(g, 64, 1) for g in gathered]
    halves = []
    for yc in range(2):
        blocks = []
        for h in range(2):
            if yc == 0:
                blocks.append(jnp.where(low96, gathered[2 * h], turned[2 * h + 1]))
            else:
                blocks.append(jnp.where(low96, turned[2 * h], gathered[2 * h + 1]))
        halves.append(
            jnp.concatenate(
                [blocks[h][8 * c : 8 * c + 8] for c in range(12) for h in range(2)], axis=1
            )
        )
    fine = jnp.concatenate(halves, axis=0).astype(BF16)
    fine = jnp.concatenate([fine] * 8, axis=0)
    products = dot_nt(vec[...], fine)

    def part_of(p):
        return own_site(lambda s: products[24 * (2 * s + p) : 24 * (2 * s + p) + 24], lane24)

    rhs = part_of(0) - times_i(part_of(1), lane24)

    def collapse(acc, keep):
        picked = jnp.where((lane96 & 32) == 0, acc[:96], acc[96:])
        if keep:
            picked = jnp.where(low96, picked, 0.0)
        rows_ref[...] = picked
        return spread_groups(own_site(lambda s: rows_ref[pl.ds(s, 24, stride=4)], lane24))

    def apply_block(u):
        w = split_field(u, lane24).astype(BF16)
        return collapse(dot(inv[...], w), True)

    solution = apply_block(rhs)
    for sweep in range(2):
        plain = split_field(solution, lane24)
        w = jnp.where(lane24 < 64, plain, swap(plain, lane24, 2))
        halo_out[sweep] = pad_rows(w)
        copies = {}
        routes = [(5, (ta, x_up)), (4, (ta, x_down)), (0, (t_down, xy))]
        if n_t > 2:
            routes.append((1, (t_up, xy)))
        routes += [(2, (base + (q + 3) % 4, xy)), (3, (base + (q + 1) % 4, xy))]
        for slot, device in routes:
            copy = pltpu.make_async_remote_copy(
                src_ref=halo_out.at[sweep],
                dst_ref=halo_in.at[sweep, slot],
                send_sem=halo_send.at[sweep, slot],
                recv_sem=halo_recv.at[sweep, slot],
                device_id=device,
                device_id_type=MESH,
            )
            copy.start()
            copies[slot] = copy
        flipped = swap(plain, lane24, 8).astype(BF16)
        acc = dot(hop[6], flipped) + dot(hop[7], flipped)
        for mu in (2, 3, 0, 1):
            slot = 0 if mu == 1 and n_t == 2 else mu
            if slot == mu:
                copies[slot].wait_recv()
            acc = acc + dot(hop[mu], halo_in[sweep, slot][:24])
        copies[4].wait_recv()
        copies[5].wait_recv()
        first_x = (lane24 & 2) == 0
        above = jnp.where(first_x, w, halo_in[sweep, 4][:24].astype(F32)).astype(BF16)
        below = jnp.where(first_x, halo_in[sweep, 5][:24].astype(F32), w).astype(BF16)
        acc_x = dot(hop[4], above) + dot(hop[5], below)
        acc = jnp.where(lanes(192) < 64, acc, acc_x)
        solution = apply_block(rhs - collapse(acc, False))
        for copy in copies.values():
            copy.wait_send()

    rounded = solution.astype(BF16).astype(F32)
    rotated = times_i(rounded, lane24)
    site = (lane24 & 2) + ((lane24 >> 3) & 1)
    columns = jnp.concatenate(
        [jnp.where(site == s, part, 0.0) for s in range(4) for part in (rounded, rotated)], axis=0
    ).astype(BF16)
    pick = (lax.broadcasted_iota(jnp.int32, (16, 128), 0) == lanes(16)).astype(F32).astype(BF16)
    coefficients = dot_nt(pick, columns).astype(BF16)
    spread = dot(coefficients, vec[...])
    for h in range(2):
        straight = []
        for yc in range(2):
            straight.append(
                jnp.concatenate(
                    [
                        spread[8 * yc : 8 * yc + 8, 256 * c + 128 * h : 256 * c + 128 * h + 128]
                        for c in range(12)
                    ],
                    axis=0,
                )
            )
        crossed = [pltpu.roll(s, 64, 1) for s in straight]
        send_back[2 * h] = jnp.where(low96, straight[0], crossed[1]).astype(BF16)
        send_back[2 * h + 1] = jnp.where(low96, crossed[0], straight[1]).astype(BF16)
    for copy in exchange(send_back, recv_back, back_send, back_recv):
        copy.wait()
    returned = jnp.concatenate(
        [dot(scatter, recv_back[zq]).astype(BF16) for zq in range(4)], axis=1
    )
    result = dot_nt(returned, perm[...])
    for xc in range(2):
        for xi in range(4):
            out_ref[4 * xc + xi] = result[48 * xc : 48 * xc + 48, 128 * xi : 128 * xi + 128]


def shards(n_ta, n_xy, residual, vectors, hopping, inverse):
    res = residual[0].transpose(0, 1, 3, 2, 4).reshape(8, 48, 128)
    vec = vectors.reshape(192, 3072)
    hop = hopping[:, :, :, :, 0, :, 0, :].transpose(0, 1, 2, 4, 5, 3).reshape(8, 192, 24)
    inv = inverse[:, :, :, 0, :, 0, :].transpose(0, 1, 3, 4, 2).reshape(192, 24)
    out = pl.pallas_call(
        functools.partial(kernel, n_ta, n_xy),
        out_shape=jax.ShapeDtypeStruct((8, 48, 128), F32),
        in_specs=[pl.BlockSpec(memory_space=pl.ANY)] * 4,
        out_specs=pl.BlockSpec(memory_space=pltpu.VMEM),
        scratch_shapes=[
            pltpu.VMEM((8, 48, 128), BF16),
            pltpu.VMEM((192, 3072), BF16),
            pltpu.VMEM((8, 192, 24), BF16),
            pltpu.VMEM((192, 24), BF16),
            pltpu.VMEM((512, 512), BF16),
            pltpu.VMEM((4, 96, 128), BF16),
            pltpu.VMEM((4, 96, 128), BF16),
            pltpu.VMEM((2, 32, 128), BF16),
            pltpu.VMEM((2, 6, 32, 128), BF16),
            pltpu.VMEM((4, 96, 128), BF16),
            pltpu.VMEM((4, 96, 128), BF16),
            pltpu.VMEM((96, 128), F32),
            pltpu.SemaphoreType.DMA((4,)),
            pltpu.SemaphoreType.DMA((3,)),
            pltpu.SemaphoreType.DMA((3,)),
            pltpu.SemaphoreType.DMA((2, 6)),
            pltpu.SemaphoreType.DMA((2, 6)),
            pltpu.SemaphoreType.DMA((3,)),
            pltpu.SemaphoreType.DMA((3,)),
        ],
        compiler_params=pltpu.CompilerParams(
            collective_id=0, has_side_effects=True, vmem_limit_bytes=32 * 1024 * 1024
        ),
    )(res, vec, hop, inv)
    return out.reshape(1, 8, 2, 12, 2, 128).transpose(0, 1, 2, 4, 3, 5)


def solution(mesh):
    placed = (
        P("ta", "xy", None, None, None, None),
        P("ta", "xy", None, None, None, None, None),
        P(None, None, None, None, "ta", "xy", None, None),
        P(None, None, None, "ta", "xy", None, None),
    )
    return jax.shard_map(
        functools.partial(shards, mesh.shape["ta"], mesh.shape["xy"]),
        mesh=mesh,
        in_specs=placed,
        out_specs=P("ta", "xy", None, None, None, None),
        check_vma=False,
    )
```

time: 134 us -> 28.1 us (0.21)
  waiting for transfers between devices: 51.6 us -> 0 us
  local copies, waits for them, and re-layouts: 43.5 us -> 4.63 us
  Pallas kernels: 0 us -> 23.2 us
  starting transfers between devices: 22.7 us -> 0 us
  matrix products: 8.23 us -> 0 us
  other arithmetic: 6.9 us -> 0 us
    ppermute x18 -> x0, waiting for transfers between devices: 51.6 us -> none  [the longest x4 39.2 us: partner(): lax.ppermute(x, axis, [(i, i ^ 1 << bit) for i in range(lax.axis_size(axi...]
    pallas_call x0 -> x1, Pallas kernels: none -> 23.2 us  [shards(): pl.pallas_call(functools.partial(kernel, n_ta, n_xy), out_shape=jax.Shape...]
    ppermute x18 -> x0, starting transfers between devices: 22.7 us -> none  [the longest x10 9.96 us: shifted(): return lax.ppermute(x, axis, [(i, (i + by) % peers) for i in range(peers)])]
    reshape x4 -> x0, local copies, waits for them, and re-layouts: 18.2 us -> none  [the longest x2 9.99 us: regroup(): return stacked.reshape(pieces.shape)]
    add x2 -> x0, local copies, waits for them, and re-layouts: 10.8 us -> none  [shards(): imag_part = products[:, :, :, :, 0, 1] + products[:, :, :, :, 1, 0]]
    sub x2 -> x0, local copies, waits for them, and re-layouts: 10.8 us -> none  [shards(): real_part = products[:, :, :, :, 0, 0] - products[:, :, :, :, 1, 1]]
    dot_general x21 -> x0, matrix products: 8.23 us -> none  [the longest x19 6.74 us: complex_apply(): jnp.einsum('pabxzy,xzyrqb->xzyrpqa', matrix, vector_field, precision=high...]
    another operation x15 -> x0, other arithmetic: 5.18 us -> none  [the longest x7 4.57 us: regroup(): stacked = jnp.stack((lower_half, upper_half), axis=section_dim)]
  transfers between devices with their start and end apart: 18 -> 0, of which waited for: 10 -> 0; matrix products, arithmetic and copies ran while one was open for 3% -> 0% of each run, Pallas kernels for 0% -> 0%
where the time goes in v1:
time: 28.1 us; the launch traced here: 27.9 us
  Pallas kernels  23.2 us (83%)
  local copies, waits for them, and re-layouts  4.63 us (16%)
    pallas_call x1, Pallas kernels, shards(): pl.pallas_call(functools.partial(kernel, n_ta, n_xy), out_shape=jax.Shape...  23.2 us
    unnamed x9, local copies, waits for them, and re-layouts  4.63 us

profile of v1, /device:TPU:0, one launch (start us, length us, event | category | flops | bytes accessed | tf_op | source)
XLA Modules:
  0.0 27.9 jit_solution(9629735938260337754)
XLA Ops:
  0.0 0.0 copy-start
  0.0 1.3 %copy-done = bf16[1,2,1,2,2,24,3072]{6,5,4,3,2,1,0:T(8,128)(2,1)S(1)} copy-done((bf16[1,2,1,2,2,24,3072]{6,5,4,3,2,1,0:T(8,128)(2,1)S(1)}, bf16[1,2,1,2,2,24,3072]{6,5,4,3,2,1,0:T(8,128)(2,1)}, u32[]{:S(2)}) %copy-start) | copy-done | bytes 1179672
  1.3 0.0 copy-start.1
  1.3 1.0 %copy-done.1 = bf16[8,2,24,24,1,2,1,2]{3,7,6,5,4,2,1,0:T(2,128)(2,1)S(1)} copy-done((bf16[8,2,24,24,1,2,1,2]{3,7,6,5,4,2,1,0:T(2,128)(2,1)S(1)}, bf16[8,2,24,24,1,2,1,2]{3,7,6,5,4,2,1,0:T(2,128)(2,1)}, u32[]{:S(2)}) %copy-start.1) | copy-done | bytes 73752
  2.3 0.0 copy-start.2
  2.3 0.9 %copy-done.2 = bf16[1,8,2,2,12,128]{5,3,4,2,1,0:T(2,128)(2,1)S(1)} copy-done((bf16[1,8,2,2,12,128]{5,3,4,2,1,0:T(2,128)(2,1)S(1)}, bf16[1,8,2,2,12,128]{5,3,4,2,1,0:T(2,128)(2,1)}, u32[]{:S(2)}) %copy-start.2) | copy-done | bytes 98328
  3.2 0.0 copy-start.3
  3.2 0.8 %copy-done.3 = bf16[2,24,24,1,2,1,2]{2,6,5,4,3,1,0:T(2,128)(2,1)S(1)} copy-done((bf16[2,24,24,1,2,1,2]{2,6,5,4,3,1,0:T(2,128)(2,1)S(1)}, bf16[2,24,24,1,2,1,2]{2,6,5,4,3,1,0:T(2,128)(2,1)}, u32[]{:S(2)}) %copy-start.3) | copy-done | bytes 9240
  4.0 23.2 %shard_map.46 = f32[8,48,128]{2,1,0:T(8,128)S(1)} custom-call(bf16[8,48,128]{2,1,0:T(8,128)(2,1)S(1)} %bitcast.22, bf16[192,3072]{1,0:T(8,128)(2,1)S(1)} %bitcast.19, bf16[8,192,24]{2,1,0:T(8,128)(2,1)S(1)} %bitcast.21, bf16[192,24]{1,0:T(8,128)(2,1)S(1)} %bitcast.23), custom_call_target="tpu_custom_call" | custom-call | tf_op jit(solution)/shard_map/pallas_call | solution.py:293
  27.2 0.7 %copy.6 = f32[1,8,2,2,12,128]{5,3,4,2,1,0:T(2,128)} copy(f32[1,8,2,2,12,128]{5,3,4,2,1,0:T(2,128)S(1)} %bitcast.20) | data formatting | bytes 393216
Async XLA Ops:
  0.0 1.3 %copy-start = (bf16[1,2,1,2,2,24,3072]{6,5,4,3,2,1,0:T(8,128)(2,1)S(1)}, bf16[1,2,1,2,2,24,3072]{6,5,4,3,2,1,0:T(8,128)(2,1)}, u32[]{:S(2)}) copy-start(bf16[1,2,1,2,2,24,3072]{6,5,4,3,2,1,0:T(8,128)(2,1)} %param.5) | copy-start | bytes 3538948
  1.3 1.0 %copy-start.1 = (bf16[8,2,24,24,1,2,1,2]{3,7,6,5,4,2,1,0:T(2,128)(2,1)S(1)}, bf16[8,2,24,24,1,2,1,2]{3,7,6,5,4,2,1,0:T(2,128)(2,1)}, u32[]{:S(2)}) copy-start(bf16[8,2,24,24,1,2,1,2]{3,7,6,5,4,2,1,0:T(2,128)(2,1)} %param.6) | copy-start | bytes 221188
  2.3 0.9 %copy-start.2 = (bf16[1,8,2,2,12,128]{5,3,4,2,1,0:T(2,128)(2,1)S(1)}, bf16[1,8,2,2,12,128]{5,3,4,2,1,0:T(2,128)(2,1)}, u32[]{:S(2)}) copy-start(bf16[1,8,2,2,12,128]{5,3,4,2,1,0:T(2,128)(2,1)} %param.4) | copy-start | bytes 294916
  3.2 0.8 %copy-start.3 = (bf16[2,24,24,1,2,1,2]{2,6,5,4,3,1,0:T(2,128)(2,1)S(1)}, bf16[2,24,24,1,2,1,2]{2,6,5,4,3,1,0:T(2,128)(2,1)}, u32[]{:S(2)}) copy-start(bf16[2,24,24,1,2,1,2]{2,6,5,4,3,1,0:T(2,128)(2,1)} %param.7) | copy-start | bytes 27652

commit v2 on v1

--- a/solution.py
+++ b/solution.py
@@ -293,7 +293,7 @@
     out = pl.pallas_call(
         functools.partial(kernel, n_ta, n_xy),
         out_shape=jax.ShapeDtypeStruct((8, 48, 128), F32),
-        in_specs=[pl.BlockSpec(memory_space=pl.ANY)] * 4,
+        in_specs=[pl.BlockSpec(memory_space=pltpu.HBM)] * 4,
         out_specs=pl.BlockSpec(memory_space=pltpu.VMEM),
         scratch_shapes=[
             pltpu.VMEM((8, 48, 128), BF16),
@@ -317,7 +317,7 @@
             pltpu.SemaphoreType.DMA((3,)),
         ],
         compiler_params=pltpu.CompilerParams(
-            collective_id=0, has_side_effects=True, vmem_limit_bytes=32 * 1024 * 1024
+            collective_id=0, has_side_effects=True, vmem_limit_bytes=63 * 1024 * 1024
         ),
     )(res, vec, hop, inv)
     return out.reshape(1, 8, 2, 12, 2, 128).transpose(0, 1, 2, 4, 3, 5)

time: 28.1 us -> 25.1 us (0.89)
  local copies, waits for them, and re-layouts: 4.63 us -> 1.62 us
    unnamed x9 -> x1, local copies, waits for them, and re-layouts: 4.63 us -> 1.62 us
where the time goes in v2:
time: 25.1 us; the launch traced here: 24.9 us
  Pallas kernels  23.3 us (93%)
  local copies, waits for them, and re-layouts  1.62 us (6%)
    pallas_call x1, Pallas kernels, shards(): pl.pallas_call(functools.partial(kernel, n_ta, n_xy), out_shape=jax.Shape...  23.3 us
    unnamed x1, local copies, waits for them, and re-layouts  1.62 us

profile of v2, /device:TPU:0, one launch (start us, length us, event | category | flops | bytes accessed | tf_op | source)
XLA Modules:
  0.0 24.9 jit_solution(1887782063836228998)
XLA Ops:
  0.0 23.3 %shard_map.46 = f32[8,48,128]{2,1,0:T(8,128)} custom-call(bf16[8,48,128]{2,1,0:T(8,128)(2,1)} %bitcast.22, bf16[192,3072]{1,0:T(8,128)(2,1)} %bitcast.19, bf16[8,192,24]{2,1,0:T(8,128)(2,1)} %bitcast.21, bf16[192,24]{1,0:T(8,128)(2,1)} %bitcast.23), custom_call_target="tpu_custom_call" | custom-call | tf_op jit(solution)/shard_map/pallas_call | solution.py:293
  23.3 1.6 %copy.6 = f32[1,8,2,2,12,128]{5,3,4,2,1,0:T(2,128)} copy(f32[1,8,2,2,12,128]{5,3,4,2,1,0:T(2,128)} %bitcast.20) | data formatting | bytes 393216

commit v3 on v2

--- a/solution.py
+++ b/solution.py
@@ -84,6 +84,7 @@
     halo_in,
     send_back,
     recv_back,
+    links,
     rows_ref,
     load_sem,
     in_send,
@@ -167,14 +168,34 @@
         return copies
 
     copies_in = exchange(send_in, recv_in, in_send, in_recv)
+    lane192 = lanes(192)
+    row192 = lax.broadcasted_iota(jnp.int32, (192, 128), 0)
+    lane24 = lanes(24)
+    row24 = lax.broadcasted_iota(jnp.int32, (24, 128), 0)
+    widen = jnp.where((lane24 >> 2) == row24, 1.0, 0.0).astype(BF16)
+    loads[3].wait()
+    blocks = jnp.where(((row192 ^ lane192) & 3) == 0, dot(inv[...], widen), 0.0).astype(BF16)
+    blocks = blocks[:, :96]
+    loads[2].wait()
+    for pack in range(2):
+        placed = jnp.zeros((192, 128), F32)
+        for m in range(4):
+            shift = jnp.where(lane24 - row24 == 32 * m, 1.0, 0.0).astype(BF16)
+            placed = placed + dot(hop[4 * pack + m], shift)
+        placed = placed.astype(BF16)
+        made = dot(blocks, jnp.concatenate([placed[:96], placed[96:]], axis=1))
+        link = jnp.concatenate(
+            [made[:96, :128] - made[96:, 128:], made[:96, 128:] + made[96:, :128]], axis=0
+        )
+        high = link.astype(BF16)
+        links[pack, 0] = high
+        links[pack, 1] = (link - high.astype(F32)).astype(BF16)
     loads[1].wait()
-    loads[2].wait()
-    loads[3].wait()
+    pending = list(copies_in)
     for copy in copies_in:
-        copy.wait()
+        copy.wait_recv()
 
     lane96 = lanes(96)
-    lane24 = lanes(24)
     low96 = lane96 < 64
     gathered = [dot(gather, recv_in[ti]) for ti in range(4)]
     turned = [pltpu.roll(g, 64, 1) for g in gathered]
@@ -207,15 +228,13 @@
         rows_ref[...] = picked
         return spread_groups(own_site(lambda s: rows_ref[pl.ds(s, 24, stride=4)], lane24))
 
-    def apply_block(u):
-        w = split_field(u, lane24).astype(BF16)
-        return collapse(dot(inv[...], w), True)
-
-    solution = apply_block(rhs)
+    started = collapse(dot(inv[...], split_field(rhs, lane24).astype(BF16)), True)
+    solution = started
     for sweep in range(2):
         plain = split_field(solution, lane24)
         w = jnp.where(lane24 < 64, plain, swap(plain, lane24, 2))
-        halo_out[sweep] = pad_rows(w)
+        wide_w = jnp.concatenate([w, jnp.zeros((8, 128), F32)], axis=0)
+        halo_out[sweep] = wide_w.astype(BF16)
         copies = {}
         routes = [(5, (ta, x_up)), (4, (ta, x_down)), (0, (t_down, xy))]
         if n_t > 2:
@@ -232,23 +251,22 @@
             )
             copy.start()
             copies[slot] = copy
-        flipped = swap(plain, lane24, 8).astype(BF16)
-        acc = dot(hop[6], flipped) + dot(hop[7], flipped)
-        for mu in (2, 3, 0, 1):
-            slot = 0 if mu == 1 and n_t == 2 else mu
-            if slot == mu:
-                copies[slot].wait_recv()
-            acc = acc + dot(hop[mu], halo_in[sweep, slot][:24])
+        flipped = pad_rows(swap(plain, lane24, 8))
+        slots = [0, 0 if n_t == 2 else 1, 2, 3]
+        for slot in (2, 3) + ((0,) if n_t == 2 else (0, 1)):
+            copies[slot].wait_recv()
+        near = jnp.concatenate([halo_in[sweep, slot] for slot in slots], axis=0)
+        acc = dot(links[0, 0], near) + dot(links[0, 1], near)
         copies[4].wait_recv()
         copies[5].wait_recv()
-        first_x = (lane24 & 2) == 0
-        above = jnp.where(first_x, w, halo_in[sweep, 4][:24].astype(F32)).astype(BF16)
-        below = jnp.where(first_x, halo_in[sweep, 5][:24].astype(F32), w).astype(BF16)
-        acc_x = dot(hop[4], above) + dot(hop[5], below)
-        acc = jnp.where(lanes(192) < 64, acc, acc_x)
-        solution = apply_block(rhs - collapse(acc, False))
-        for copy in copies.values():
-            copy.wait_send()
+        first_x = (lanes(32) & 2) == 0
+        above = jnp.where(first_x, wide_w, halo_in[sweep, 4].astype(F32)).astype(BF16)
+        below = jnp.where(first_x, halo_in[sweep, 5].astype(F32), wide_w).astype(BF16)
+        far = jnp.concatenate([above, below, flipped, flipped], axis=0)
+        acc_far = dot(links[1, 0], far) + dot(links[1, 1], far)
+        acc = jnp.where(lane192 < 64, acc, acc_far)
+        solution = started - collapse(acc, False)
+        pending += list(copies.values())
 
     rounded = solution.astype(BF16).astype(F32)
     rotated = times_i(rounded, lane24)
@@ -274,15 +292,19 @@
         crossed = [pltpu.roll(s, 64, 1) for s in straight]
         send_back[2 * h] = jnp.where(low96, straight[0], crossed[1]).astype(BF16)
         send_back[2 * h + 1] = jnp.where(low96, crossed[0], straight[1]).astype(BF16)
-    for copy in exchange(send_back, recv_back, back_send, back_recv):
-        copy.wait()
+    copies_back = exchange(send_back, recv_back, back_send, back_recv)
+    pending += copies_back
+    for copy in copies_back:
+        copy.wait_recv()
     returned = jnp.concatenate(
         [dot(scatter, recv_back[zq]).astype(BF16) for zq in range(4)], axis=1
     )
-    result = dot_nt(returned, perm[...])
+    result = dot_nt(returned, perm[...]).astype(BF16)
     for xc in range(2):
         for xi in range(4):
             out_ref[4 * xc + xi] = result[48 * xc : 48 * xc + 48, 128 * xi : 128 * xi + 128]
+    for copy in pending:
+        copy.wait_send()
 
 
 def shards(n_ta, n_xy, residual, vectors, hopping, inverse):
@@ -292,7 +314,7 @@
     inv = inverse[:, :, :, 0, :, 0, :].transpose(0, 1, 3, 4, 2).reshape(192, 24)
     out = pl.pallas_call(
         functools.partial(kernel, n_ta, n_xy),
-        out_shape=jax.ShapeDtypeStruct((8, 48, 128), F32),
+        out_shape=jax.ShapeDtypeStruct((8, 48, 128), BF16),
         in_specs=[pl.BlockSpec(memory_space=pltpu.HBM)] * 4,
         out_specs=pl.BlockSpec(memory_space=pltpu.VMEM),
         scratch_shapes=[
@@ -307,6 +329,7 @@
             pltpu.VMEM((2, 6, 32, 128), BF16),
             pltpu.VMEM((4, 96, 128), BF16),
             pltpu.VMEM((4, 96, 128), BF16),
+            pltpu.VMEM((2, 2, 192, 128), BF16),
             pltpu.VMEM((96, 128), F32),
             pltpu.SemaphoreType.DMA((4,)),
             pltpu.SemaphoreType.DMA((3,)),
@@ -320,7 +343,7 @@
             collective_id=0, has_side_effects=True, vmem_limit_bytes=63 * 1024 * 1024
         ),
     )(res, vec, hop, inv)
-    return out.reshape(1, 8, 2, 12, 2, 128).transpose(0, 1, 2, 4, 3, 5)
+    return out.astype(F32).reshape(1, 8, 2, 12, 2, 128).transpose(0, 1, 2, 4, 3, 5)
 
 
 def solution(mesh):

time: 25.1 us -> 24.3 us (0.968)
  local copies, waits for them, and re-layouts: 1.62 us -> 0 us
  other arithmetic: 0 us -> 1.58 us
  Pallas kernels: 23.3 us -> 22.5 us
    unnamed x1 -> x0, local copies, waits for them, and re-layouts: 1.62 us -> none
    unnamed x0 -> x1, other arithmetic: none -> 1.58 us
    pallas_call x1, Pallas kernels: 23.3 us -> 22.5 us  [shards(): pl.pallas_call(functools.partial(kernel, n_ta, n_xy), out_shape=jax.Shape...]
where the time goes in v3:
time: 24.3 us; the launch traced here: 24.1 us
  Pallas kernels  22.5 us (93%)
  other arithmetic  1.58 us (7%)
    pallas_call x1, Pallas kernels, shards(): pl.pallas_call(functools.partial(kernel, n_ta, n_xy), out_shape=jax.Shape...  22.5 us
    unnamed x1, other arithmetic  1.58 us

profile of v3, /device:TPU:0, one launch (start us, length us, event | category | flops | bytes accessed | tf_op | source)
XLA Modules:
  0.0 24.1 jit_solution(2934093011277184234)
XLA Ops:
  0.0 22.5 %shard_map.46 = bf16[8,48,128]{2,1,0:T(8,128)(2,1)} custom-call(bf16[8,48,128]{2,1,0:T(8,128)(2,1)} %bitcast.25, bf16[192,3072]{1,0:T(8,128)(2,1)} %bitcast.22, bf16[8,192,24]{2,1,0:T(8,128)(2,1)} %bitcast.23, bf16[192,24]{1,0:T(8,128)(2,1)} %bitcast.26), custom_call_target="tpu_custom_call" | custom-call | tf_op jit(solution)/shard_map/pallas_call | solution.py:315
  22.5 1.6 %convert.5 = f32[8,48,128]{2,1,0:T(8,128)} convert(bf16[8,48,128]{2,1,0:T(8,128)(2,1)} %shard_map.46) | non-fusion elementwise | flops 49152 | bytes 294912

commit v4 on v3

--- a/solution.py
+++ b/solution.py
@@ -100,23 +100,25 @@
     base = ta - q
     n_t = n_ta // 4
 
-    loads = []
-    for i, (src, dst) in enumerate(((res_hbm, res), (vec_hbm, vec), (hop_hbm, hop), (inv_hbm, inv))):
-        copy = pltpu.make_async_copy(src, dst, load_sem.at[i])
-        copy.start()
-        loads.append(copy)
-
     t_up = (ta + 4) % n_ta
     t_down = (ta + n_ta - 4) % n_ta
     x_up = (xy + 1) % n_xy
     x_down = (xy + n_xy - 1) % n_xy
-    mates = [base + (q + j) % 4 for j in (1, 2, 3)]
+    beside = q + 1 - 2 * (q % 2)
+    slots_of_mates = ((q + 2) % 4, (beside + 2) % 4, beside)
+    mates = [base + slot for slot in slots_of_mates]
     greeted = [(mate, xy) for mate in mates] + [(ta, x_up), (ta, x_down), (t_up, xy)]
     if n_t > 2:
         greeted.append((t_down, xy))
     barrier = pltpu.get_barrier_semaphore()
     for device in greeted:
         pl.semaphore_signal(barrier, inc=1, device_id=device, device_id_type=MESH)
+
+    loads = [
+        pltpu.make_async_copy(src, dst, load_sem.at[i])
+        for i, (src, dst) in enumerate(((res_hbm, res), (vec_hbm, vec), (hop_hbm, hop), (inv_hbm, inv)))
+    ]
+    loads[0].start()
 
     row128 = lax.broadcasted_iota(jnp.int32, (128, 128), 0)
     col128 = lanes(128)
@@ -137,6 +139,8 @@
     scatter = jnp.where(r96 == fine_row(c96), 1.0, 0.0).astype(BF16)
 
     loads[0].wait()
+    for copy in (loads[3], loads[2], loads[1]):
+        copy.start()
     wide = jnp.concatenate(
         [
             jnp.concatenate([res[4 * xc + xi] for xi in range(4)], axis=1)
@@ -152,13 +156,12 @@
 
     def exchange(src, dst, send_sem, recv_sem):
         copies = []
-        for j in (2, 3, 1):
-            slot = (q + j) % 4
+        for j, slot in enumerate(slots_of_mates):
             copy = pltpu.make_async_remote_copy(
                 src_ref=src.at[slot],
                 dst_ref=dst.at[q],
-                send_sem=send_sem.at[j - 1],
-                recv_sem=recv_sem.at[j - 1],
+                send_sem=send_sem.at[j],
+                recv_sem=recv_sem.at[j],
                 device_id=(base + slot, xy),
                 device_id_type=MESH,
             )
@@ -299,7 +302,7 @@
     returned = jnp.concatenate(
         [dot(scatter, recv_back[zq]).astype(BF16) for zq in range(4)], axis=1
     )
-    result = dot_nt(returned, perm[...]).astype(BF16)
+    result = dot_nt(returned, perm[...])
     for xc in range(2):
         for xi in range(4):
             out_ref[4 * xc + xi] = result[48 * xc : 48 * xc + 48, 128 * xi : 128 * xi + 128]
@@ -314,7 +317,7 @@
     inv = inverse[:, :, :, 0, :, 0, :].transpose(0, 1, 3, 4, 2).reshape(192, 24)
     out = pl.pallas_call(
         functools.partial(kernel, n_ta, n_xy),
-        out_shape=jax.ShapeDtypeStruct((8, 48, 128), BF16),
+        out_shape=pltpu.VMEM((8, 48, 128), F32),
         in_specs=[pl.BlockSpec(memory_space=pltpu.HBM)] * 4,
         out_specs=pl.BlockSpec(memory_space=pltpu.VMEM),
         scratch_shapes=[
@@ -340,10 +343,10 @@
             pltpu.SemaphoreType.DMA((3,)),
         ],
         compiler_params=pltpu.CompilerParams(
-            collective_id=0, has_side_effects=True, vmem_limit_bytes=63 * 1024 * 1024
+            collective_id=0, has_side_effects=True, vmem_limit_bytes=56 * 1024 * 1024
         ),
     )(res, vec, hop, inv)
-    return out.astype(F32).reshape(1, 8, 2, 12, 2, 128).transpose(0, 1, 2, 4, 3, 5)
+    return out.reshape(1, 8, 2, 12, 2, 128).transpose(0, 1, 2, 4, 3, 5)
 
 
 def solution(mesh):

time: 24.3 us -> 22.7 us (0.934)
  other arithmetic: 1.58 us -> 0 us
  local copies, waits for them, and re-layouts: 0 us -> 0.68 us
  Pallas kernels: 22.5 us -> 21.9 us
    unnamed x1 -> x0, other arithmetic: 1.58 us -> none
    unnamed x0 -> x1, local copies, waits for them, and re-layouts: none -> 0.68 us
    pallas_call x1, Pallas kernels: 22.5 us -> 21.9 us  [shards(): pl.pallas_call(functools.partial(kernel, n_ta, n_xy), out_shape=pltpu.VME...]
where the time goes in v4:
time: 22.7 us; the launch traced here: 22.6 us
  Pallas kernels  21.9 us (96%)
  local copies, waits for them, and re-layouts  0.68 us (3%)
    pallas_call x1, Pallas kernels, shards(): pl.pallas_call(functools.partial(kernel, n_ta, n_xy), out_shape=pltpu.VME...  21.9 us
    unnamed x1, local copies, waits for them, and re-layouts  0.68 us

profile of v4, /device:TPU:0, one launch (start us, length us, event | category | flops | bytes accessed | tf_op | source)
XLA Modules:
  0.0 22.6 jit_solution(9263871280615319516)
XLA Ops:
  0.0 21.9 %shard_map.46 = f32[8,48,128]{2,1,0:T(8,128)S(1)} custom-call(bf16[8,48,128]{2,1,0:T(8,128)(2,1)} %bitcast.22, bf16[192,3072]{1,0:T(8,128)(2,1)} %bitcast.20, bf16[8,192,24]{2,1,0:T(8,128)(2,1)} %bitcast.21, bf16[192,24]{1,0:T(8,128)(2,1)} %bitcast.23), custom_call_target="tpu_custom_call" | custom-call | tf_op jit(solution)/shard_map/pallas_call | solution.py:318
  21.9 0.7 %copy.6 = f32[1,8,2,2,12,128]{5,3,4,2,1,0:T(2,128)} copy(f32[1,8,2,2,12,128]{5,3,4,2,1,0:T(2,128)S(1)} %bitcast.19) | data formatting | bytes 393216
